TPU v7x, 256 devices: a whole 4x4x8 slice. The times are simulated.
256 devices in a mesh: row: 8 (over y, x_hi), col: 32 (over z, x_lo, core).
Axes of the slice: x: 4 (x_hi: 2, x_lo: 2; x = x_hi * 2 + x_lo), y: 4, z: 8, core: 2. Of those that a mesh axis runs over, the one named last changes fastest.
Arguments:
- activations: bfloat16 [256, 8192], P(None, 'col'), may hold values from -6 to 6
- out_grads: bfloat16 [256, 28672], P('col', 'row'), may hold values from -6 to 6
- input_basis: bfloat16 [8192, 8192], P('col', 'row'), may hold values from -0.0625 to 0.0625
- output_basis: bfloat16 [28672, 28672], P('row', 'col'), may hold values from -0.03125 to 0.03125
- eigenvalues: float32 [8192, 28672], P('row', 'col'), may hold values from 0.05 to 5
- query_inputs: bfloat16 [512, 8192], P(None, 'row'), may hold values from -0.015625 to 0.015625
- query_outgrads: bfloat16 [512, 28672], P(None, 'col'), may hold values from -0.0078125 to 0.0078125
Outputs:
- scores: float32 [32, 16], replicated
All inputs are finite; a program needn't handle non-finite values.
Results may differ from a plain program's by a relative error of at most 0.0059.
Values may be sent and summed in bfloat16 or wider, within the bound.
A program may use at most 192 MiB of HBM per device.

v0:
```python
import math

import jax
import jax.numpy as jnp
from jax import lax
from jax.sharding import PartitionSpec as P

SEQS = 16
TOK = 16
QUERIES = 32
QTOK = 16


damping = 0.05


def per_device(
    activations, out_grads, input_basis, output_basis, eigenvalues, query_inputs, query_outgrads
):
    in_terms = jnp.dot(activations, input_basis, preferred_element_type=jnp.float32)
    rotated_in = lax.psum(in_terms, "col").astype(jnp.bfloat16)
    out_terms = jnp.dot(
        lax.all_gather(out_grads, "col", axis=0, tiled=True),
        output_basis,
        preferred_element_type=jnp.float32,
    )
    rotated_out = lax.psum(out_terms, "row").astype(jnp.bfloat16)
    seq_in = rotated_in.reshape(SEQS, TOK, rotated_in.shape[1])
    seq_out = rotated_out.reshape(SEQS, TOK, rotated_out.shape[1])
    shifted = eigenvalues + damping

    def precondition(pair):
        grad = jnp.einsum("ti,tj->ij", pair[0], pair[1], preferred_element_type=jnp.float32)
        return (grad / shifted).astype(jnp.bfloat16)

    scaled = lax.map(precondition, (seq_in, seq_out))
    group = math.gcd(QUERIES, 8)
    query_in = query_inputs.reshape(QUERIES // group, group, QTOK, query_inputs.shape[1])
    query_out = query_outgrads.reshape(QUERIES // group, group, QTOK, query_outgrads.shape[1])

    def score_group(pair):
        query_grad = jnp.einsum(
            "qti,qtj->qij", pair[0], pair[1], preferred_element_type=jnp.float32
        ).astype(jnp.bfloat16)
        return jnp.einsum("qij,sij->qs", query_grad, scaled, preferred_element_type=jnp.float32)

    partial_scores = lax.map(score_group, (query_in, query_out)).reshape(QUERIES, SEQS)
    return lax.psum(partial_scores, ("row", "col"))


def solution(mesh):
    in_specs = (
        P(None, "col"),
        P("col", "row"),
        P("col", "row"),
        P("row", "col"),
        P("row", "col"),
        P(None, "row"),
        P(None, "col"),
    )
    out_specs = P()
    return jax.shard_map(
        per_device, mesh=mesh, in_specs=in_specs, out_specs=out_specs, check_vma=False
    )
```

profile of v0, /device:TPU:1, one launch (start us, length us, event | category | flops | bytes accessed | tf_op | source)
XLA Modules:
  0.0 504.1 jit_solution(12169939148539186306)
XLA Ops:
  8.8 4.2 broadcast_add_fusion
  12.9 118.7 %all-reduce.2 = bf16[256,1024]{1,0:T(8,128)(2,1)S(1)} all-reduce(f32[256,1024]{1,0:T(8,128)S(1)} %fusion.14), channel_id=1, replica_groups=mesh['row'=8,'col'=32] {'col'}, use_global_device_ids=true, to_apply=%region_0.0 | all-reduce | flops 262144 | bytes 1572864 | tf_op jit(solution)/shard_map/psum | solution.py:21
  131.6 5.5 %fusion.15 = f32[256,896]{1,0:T(8,128)S(1)} fusion(bf16[256,3584]{1,0:T(8,128)(2,1)} %all-gather.2.cloned.1.call-done, bf16[3584,896]{1,0:T(8,128)(2,1)} %param.14), kind=kOutput, calls=%fused_computation.19 | convolution fusion | flops 1644167168 | bytes 9175040 | tf_op jit(solution)/shard_map/dot_general | solution.py:22
  137.1 50.9 %all-reduce.3 = bf16[256,896]{1,0:T(8,128)(2,1)S(1)} all-reduce(f32[256,896]{1,0:T(8,128)S(1)} %fusion.15), channel_id=1, replica_groups=mesh['row'=8,'col'=32] {'row'}, use_global_device_ids=true, to_apply=%region_1.0 | all-reduce | flops 229376 | bytes 1376256 | tf_op jit(solution)/shard_map/psum | solution.py:27
  188.0 63.7 %while.20 = (s32[]{:T(128)}, bf16[16,1024,896]{2,1,0:T(8,128)(2,1)}, bf16[16,16,1024]{2,1,0:T(8,128)(2,1)S(1)}, bf16[16,16,896]{2,1,0:T(8,128)(2,1)S(1)}, f32[1024,896]{1,0:T(8,128)}, /*index=5*/s32[]{:T(128)}) while((s32[]{:T(128)}, bf16[16,1024,896]{2,1,0:T(8,128)(2,1)}, bf16[16,16,1024]{2,1,0:T(8,128)(2,1)S(1)}, ...), condition=%wide.region_3.4_spmd, body=%wide.region_2.3_spmd.sunk | while | flops 31195136 | bytes 5568069 | solution.py:36
  188.0 4.0 bitcast_dynamic-update-slice_fusion.2
  191.9 3.9 bitcast_dynamic-update-slice_fusion.2
  195.9 4.0 bitcast_dynamic-update-slice_fusion.2
  199.9 4.0 bitcast_dynamic-update-slice_fusion.2
  203.9 4.0 bitcast_dynamic-update-slice_fusion.2
  207.9 4.0 bitcast_dynamic-update-slice_fusion.2
  211.9 4.0 bitcast_dynamic-update-slice_fusion.2
  215.8 4.0 bitcast_dynamic-update-slice_fusion.2
  219.8 4.0 bitcast_dynamic-update-slice_fusion.2
  223.8 4.0 bitcast_dynamic-update-slice_fusion.2
  227.7 3.9 bitcast_dynamic-update-slice_fusion.2
  231.7 4.0 bitcast_dynamic-update-slice_fusion.2
  235.7 4.0 bitcast_dynamic-update-slice_fusion.2
  239.7 4.0 bitcast_dynamic-update-slice_fusion.2
  243.7 4.0 bitcast_dynamic-update-slice_fusion.2
  247.7 3.9 bitcast_dynamic-update-slice_fusion.2
  251.6 26.2 %copy.10 = bf16[16,1024,896]{2,0,1:T(8,128)(2,1)} copy(bf16[16,1024,896]{2,1,0:T(8,128)(2,1)} %get-tuple-element.70) | data formatting | bytes 58720256 | tf_op jit(solution)/shard_map/while | solution.py:47
  277.9 137.9 %while.21 = (s32[]{:T(128)}, f32[4,8,16]{2,1,0:T(8,128)S(1)}, bf16[4,8,16,1024]{3,2,1,0:T(8,128)(2,1)}, bf16[4,8,16,896]{3,2,1,0:T(8,128)(2,1)}, bf16[16,1024,896]{2,0,1:T(8,128)(2,1)}, /*index=5*/s32[]{:T(128)}) while((s32[]{:T(128)}, f32[4,8,16]{2,1,0:T(8,128)S(1)}, bf16[4,8,16,1024]{3,2,1,0:T(8,128)(2,1)}, ...), condition=%wide.region_5.6_spmd, body=%wide.region_4.5_spmd.sunk | while | flops 469762048 | bytes 59216968 | solution.py:47
  277.9 10.2 %fusion.33 = bf16[8,1024,896]{2,1,0:T(8,128)(2,1)} fusion(bf16[4,8,16,1024]{3,2,1,0:T(8,128)(2,1)} %get-tuple-element.185, s32[]{:T(128)} %get-tuple-element.177, bf16[4,8,16,896]{3,2,1,0:T(8,128)(2,1)} %get-tuple-element.186), kind=kOutput, calls=%fused_computation.11.clone.1 | convolution fusion | flops 234881024 | bytes 15172608 | tf_op jit(solution)/shard_map/while/body/eval_jaxpr/qti,qtj->qij/dot_general | solution.py:42
  288.1 24.2 %fusion.34 = f32[4,8,16]{2,1,0:T(8,128)S(1)} fusion(f32[4,8,16]{2,1,0:T(8,128)S(1)} %get-tuple-element.178, s32[]{:T(128)} %get-tuple-element.177, bf16[16,1024,896]{2,0,1:T(8,128)(2,1)} %get-tuple-element.187, bf16[8,1024,896]{2,1,0:T(8,128)(2,1)} %fusion.33), kind=kOutput, calls=%fused_computation.10.clone.1 | convolution fusion | flops 234881024 | bytes 44044292 | tf_op jit(solution)/shard_map/while/body/eval_jaxpr/qij,sij->qs/dot_general | solution.py:45
  312.4 10.2 %fusion.33 = bf16[8,1024,896]{2,1,0:T(8,128)(2,1)} fusion(bf16[4,8,16,1024]{3,2,1,0:T(8,128)(2,1)} %get-tuple-element.185, s32[]{:T(128)} %get-tuple-element.177, bf16[4,8,16,896]{3,2,1,0:T(8,128)(2,1)} %get-tuple-element.186), kind=kOutput, calls=%fused_computation.11.clone.1 | convolution fusion | flops 234881024 | bytes 15172608 | tf_op jit(solution)/shard_map/while/body/eval_jaxpr/qti,qtj->qij/dot_general | solution.py:42
  322.6 24.2 %fusion.34 = f32[4,8,16]{2,1,0:T(8,128)S(1)} fusion(f32[4,8,16]{2,1,0:T(8,128)S(1)} %get-tuple-element.178, s32[]{:T(128)} %get-tuple-element.177, bf16[16,1024,896]{2,0,1:T(8,128)(2,1)} %get-tuple-element.187, bf16[8,1024,896]{2,1,0:T(8,128)(2,1)} %fusion.33), kind=kOutput, calls=%fused_computation.10.clone.1 | convolution fusion | flops 234881024 | bytes 44044292 | tf_op jit(solution)/shard_map/while/body/eval_jaxpr/qij,sij->qs/dot_general | solution.py:45
  346.8 10.2 %fusion.33 = bf16[8,1024,896]{2,1,0:T(8,128)(2,1)} fusion(bf16[4,8,16,1024]{3,2,1,0:T(8,128)(2,1)} %get-tuple-element.185, s32[]{:T(128)} %get-tuple-element.177, bf16[4,8,16,896]{3,2,1,0:T(8,128)(2,1)} %get-tuple-element.186), kind=kOutput, calls=%fused_computation.11.clone.1 | convolution fusion | flops 234881024 | bytes 15172608 | tf_op jit(solution)/shard_map/while/body/eval_jaxpr/qti,qtj->qij/dot_general | solution.py:42
  357.1 24.2 %fusion.34 = f32[4,8,16]{2,1,0:T(8,128)S(1)} fusion(f32[4,8,16]{2,1,0:T(8,128)S(1)} %get-tuple-element.178, s32[]{:T(128)} %get-tuple-element.177, bf16[16,1024,896]{2,0,1:T(8,128)(2,1)} %get-tuple-element.187, bf16[8,1024,896]{2,1,0:T(8,128)(2,1)} %fusion.33), kind=kOutput, calls=%fused_computation.10.clone.1 | convolution fusion | flops 234881024 | bytes 44044292 | tf_op jit(solution)/shard_map/while/body/eval_jaxpr/qij,sij->qs/dot_general | solution.py:45
  381.3 10.2 %fusion.33 = bf16[8,1024,896]{2,1,0:T(8,128)(2,1)} fusion(bf16[4,8,16,1024]{3,2,1,0:T(8,128)(2,1)} %get-tuple-element.185, s32[]{:T(128)} %get-tuple-element.177, bf16[4,8,16,896]{3,2,1,0:T(8,128)(2,1)} %get-tuple-element.186), kind=kOutput, calls=%fused_computation.11.clone.1 | convolution fusion | flops 234881024 | bytes 15172608 | tf_op jit(solution)/shard_map/while/body/eval_jaxpr/qti,qtj->qij/dot_general | solution.py:42
  391.6 24.2 %fusion.34 = f32[4,8,16]{2,1,0:T(8,128)S(1)} fusion(f32[4,8,16]{2,1,0:T(8,128)S(1)} %get-tuple-element.178, s32[]{:T(128)} %get-tuple-element.177, bf16[16,1024,896]{2,0,1:T(8,128)(2,1)} %get-tuple-element.187, bf16[8,1024,896]{2,1,0:T(8,128)(2,1)} %fusion.33), kind=kOutput, calls=%fused_computation.10.clone.1 | convolution fusion | flops 234881024 | bytes 44044292 | tf_op jit(solution)/shard_map/while/body/eval_jaxpr/qij,sij->qs/dot_general | solution.py:45
  415.8 80.8 %psum.23 = f32[32,16]{1,0:T(8,128)S(1)} all-reduce(f32[32,16]{1,0:T(8,128)S(1)} %bitcast.47), channel_id=1, replica_groups=mesh['row'=8,'col'=32] {'row','col'}, use_global_device_ids=true, to_apply=%region_6.7 | all-reduce | flops 512 | bytes 4096 | tf_op jit(solution)/shard_map/psum | solution.py:48
  (11 shorter events, 2.9 us)
Async XLA Ops:
  6.5 1.0 copy-start
  6.5 125.1 %all-gather.2.cloned.1.call-start = ((), (), s32[]{:S(2)}) async-start(), calls=%async_computation | async-start | bytes 1892352 | tf_op jit(solution)/shard_map/all_gather | solution.py:23
  415.8 81.5 %copy-start.1 = (bf16[256,1024]{1,0:T(8,128)(2,1)S(1)}, bf16[256,1024]{1,0:T(8,128)(2,1)}, u32[]{:S(2)}) copy-start(bf16[256,1024]{1,0:T(8,128)(2,1)} %param.13) | copy-start | bytes 1572868
Sparse Core Ops, SparseCore 0:
  9.2 68.7 all-gather.1
where the time goes:
time: 505 us; the launch traced here: 504 us
  blocking collectives  250 us (50%)
  matrix products  208 us (41%)
  local copies, waits for them, and re-layouts  27.2 us (5%)
  between operations  13.4 us (3%)
    psum x1, blocking collectives, per_device(): rotated_in = lax.psum(in_terms, 'col').astype(jnp.bfloat16)  119 us
    dot_general x4, matrix products, score_group(): jnp.einsum('qij,sij->qs', query_grad, scaled, preferred_element_type=jnp....  97 us
    psum x1, blocking collectives, per_device(): return lax.psum(partial_scores, ('row', 'col'))  80.8 us
    dot_general x16, matrix products, precondition(): jnp.einsum('ti,tj->ij', pair[0], pair[1], preferred_element_type=jnp.floa...  63.6 us
    psum x1, blocking collectives, per_device(): rotated_out = lax.psum(out_terms, 'row').astype(jnp.bfloat16)  50.9 us
    dot_general x4, matrix products, score_group(): jnp.einsum('qti,qtj->qij', pair[0], pair[1], preferred_element_type=jnp.f...  40.9 us
    while x1, local copies, waits for them, and re-layouts, per_device(): lax.map(score_group, (query_in, query_out)).reshape(QUERIES, SEQS)  26.2 us
  transfers between devices with their start and end apart: 1, of which 0 were waited for; matrix products, arithmetic and copies ran while one was open for 1% of the time, Pallas kernels for 0%

commit v1 on v0

v1 whole, which is shorter than its diff:
```python
import functools

import jax
import jax.numpy as jnp
from jax import lax
from jax.experimental import pallas as pl
from jax.experimental.pallas import tpu as pltpu
from jax.sharding import PartitionSpec as P

MESH = pl.DeviceIdType.MESH
F32, BF16, F8 = jnp.float32, jnp.bfloat16, jnp.float8_e4m3fn

D_I, D_J = 1024, 896
TOKENS, QUERIES, QTOK, SEQS = 256, 32, 16, 16
HALF = 1792
POOL = 14
DAMPING = 0.05
ORDER = (1, 7, 2, 6, 3, 5, 4)

RI_CORE, RI_X, RI_RS, RI_AG, RI_AGX, RI_AGC = 0, 1, 2, 9, 16, 17
OG_CORE, OG_Z, OG_X, OG_C = 18, 19, 26, 34
RO_RS, RO_AG = 50, 57
AR_C, AR_XY, AR_Z = 64, 65, 80
N_SEMS = 87


def power_scale(peak, top):
    scale = jnp.full_like(peak, 256.0 / top)
    for k in range(1, 15):
        scale = jnp.where(peak <= top * 0.25**k, 256.0 / top * 4.0**k, scale)
    return scale


def split8(x, top):
    scale = power_scale(jnp.max(jnp.abs(x), axis=(0, 1), keepdims=True), top)
    x = x * scale
    high = x.astype(F8).astype(F32)
    return high, x - high, scale


def kernel(
    act, ib, og, qi, qo, eig, ob, out,
    act_v, ib_v, qi_v, qo_v, eig_v, wt, qa, qb, scl, pool, ma, mb, pst,
    rip, r1, acc1, s2, r2, s3, s3f, r3, rig, riv,
    ogx, ogr, ogg, rop, ror, rog, rot, sc, ar_s, ar_r,
    lsem, ssem, rsem,
):
    row, col = lax.axis_index("row"), lax.axis_index("col")
    z, low = lax.div(col, 4), lax.rem(col, 4)
    xl, k = lax.div(low, 2), lax.rem(low, 2)
    core_peer = (row, col + 1 - 2 * k)
    x_col = z * 4 + lax.rem(low + 2, 4)
    x_peer = (row, x_col)

    def z_peer(d):
        return (row, lax.rem(z + d, 8) * 4 + low)

    def row_peer(d):
        return (lax.rem(row + d, 8), col)

    xy = [(d, e) for d in range(8) for e in range(2) if d or e]

    def xy_peer(d, e):
        return (lax.rem(row + d, 8), x_col if e else col)

    barrier = pltpu.get_barrier_semaphore()
    peers = [core_peer] + [z_peer(d) for d in range(1, 8)] + [xy_peer(d, e) for d, e in xy]
    for p in peers:
        pl.semaphore_signal(barrier, inc=1, device_id=p, device_id_type=MESH)

    started = []

    def send(src, dst, sem, peer):
        c = pltpu.make_async_remote_copy(
            src_ref=src, dst_ref=dst, send_sem=ssem.at[sem], recv_sem=rsem.at[sem],
            device_id=peer, device_id_type=MESH,
        )
        c.start()
        started.append(c)
        return c

    def fetch(src, dst, sem):
        c = pltpu.make_async_copy(src, dst, lsem.at[sem])
        c.start()
        return c

    ob_v = pool.at[pl.ds(0, 2 * HALF), pl.ds(0, D_J)]
    get_act = fetch(act, act_v, 0)
    get_ib = fetch(ib, ib_v, 1)
    get_eig = [fetch(eig.at[pl.ds(256 * c, 256)], eig_v.at[c % 2], 2 + c) for c in range(2)]
    get_qi = fetch(qi, qi_v, 6)
    get_qo = fetch(qo, qo_v, 7)

    own_og = og[...].astype(F32)
    ogx[0] = own_og[:, :HALF]
    ogx[1] = own_og[:, HALF:]

    get_act.wait()
    get_ib.wait()
    part = jnp.dot(act_v[...], ib_v[...], preferred_element_type=F32)
    rip[...] = part

    for c in range(4):
        get_eig[c].wait()
        wt[:, pl.ds(256 * c, 256)] = 1.0 / (eig_v[c % 2].T + DAMPING)
        if c < 2:
            get_eig.append(fetch(eig.at[pl.ds(256 * (c + 2), 256)], eig_v.at[c % 2], 4 + c))
    get_ob = fetch(ob, ob_v, 8)
    get_qi.wait()
    get_qo.wait()

    pl.semaphore_wait(barrier, len(peers))

    ri_c = send(
        rip.at[pl.ds(pl.multiple_of(128 - 128 * k, 128), 128), :], r1, RI_CORE, core_peer
    )
    og_c = send(ogx.at[1 - k], ogr, OG_CORE, core_peer)

    def prepare(pair, carry):
        sides = []
        for e in range(2):
            q = 2 * pair + e
            rows = pl.ds(pl.multiple_of(q * QTOK, QTOK), QTOK)
            high, rest, a = split8(qi_v[rows, :].astype(F32), 2.0**-6)
            used = jnp.concatenate([high, rest, high, rest], axis=0)
            none = jnp.zeros_like(used)
            qb[q] = jnp.concatenate([none, used] if e else [used, none], axis=0).astype(F8)
            high, rest, b = split8(qo_v[rows, :].astype(F32), 2.0**-7)
            sides.append(jnp.concatenate([high, high, rest, rest], axis=0))
            scl[pl.ds(q, 1), :] = jnp.broadcast_to(1.0 / (a * b), (1, TOKENS))
        both = jnp.concatenate(sides, axis=0).astype(BF16)
        qa[pair] = both.T.astype(F32).astype(F8)
        return carry

    def weighted(q):
        g = jnp.dot(qa[lax.div(q, 2)], qb[q], preferred_element_type=F32)
        return (g * wt[...]).astype(BF16)

    def fill(slot, carry):
        rows = pl.ds(pl.multiple_of(slot * D_J, D_J), D_J)
        pool[rows, :] = weighted(slot)
        return carry

    lax.fori_loop(0, 4, prepare, 0)

    ri_c.wait_recv()
    acc = rip[pl.ds(pl.multiple_of(128 * k, 128), 128), :] + r1[...]
    acc1[...] = acc
    s2[0] = acc[:64].astype(BF16)
    s2[1] = acc[64:].astype(BF16)
    ri_x = send(s2.at[1 - xl], r2, RI_X, x_peer)

    og_c.wait_recv()
    mine = ogx[k]
    other = ogr[...]
    first = jnp.where(k == 0, mine, other)
    second = jnp.where(k == 0, other, mine)
    own_seq = 2 * z + xl
    ogg[k, own_seq] = jnp.concatenate([first, second], axis=0).astype(BF16)

    def og_send(n):
        d = ORDER[n]
        block = ogg.at[k, own_seq]
        return send(block, block, OG_Z + n, z_peer(d))

    og_z = [og_send(n) for n in range(4)]
    og_x, og_f = [], []

    def og_forward(n):
        if n:
            og_z[n - 1].wait_recv()
            d = ORDER[n - 1]
            block = ogg.at[k, 2 * lax.rem(z + 8 - d, 8) + xl]
        else:
            block = ogg.at[k, own_seq]
        og_x.append(send(block, block, OG_X + n, x_peer))
        og_f.append(send(block, block, OG_C + n, core_peer))

    def og_forward_x(n):
        og_x[n].wait_recv()
        d = ORDER[n - 1] if n else 0
        block = ogg.at[k, 2 * lax.rem(z + 8 - d, 8) + 1 - xl]
        og_f.append(send(block, block, OG_C + 8 + n, core_peer))

    og_forward(0)
    lax.fori_loop(4, 16, prepare, 0)

    ri_x.wait_recv()
    acc = acc1[pl.ds(pl.multiple_of(64 * xl, 64), 64), :] + r2[...].astype(F32)
    for c in range(8):
        piece = acc[16 * (c % 4) : 16 * (c % 4) + 16, 512 * (c // 4) : 512 * (c // 4) + 512]
        s3f[c] = piece
        s3[c] = piece.astype(BF16)
    ri_rs = [send(s3.at[lax.rem(z + d, 8)], r3.at[d], RI_RS + d - 1, z_peer(d)) for d in range(1, 8)]
    og_z += [og_send(n) for n in range(4, 7)]

    lax.fori_loop(4, 9, fill, 0)
    for n in range(1, 5):
        og_forward(n)

    for c in ri_rs:
        c.wait_recv()
    total = s3f[z]
    for d in range(1, 8):
        total = total + r3[d].astype(F32)
    rig[k, xl, z] = total.astype(BF16)
    block = rig.at[k, xl, z]
    ri_ag = [send(block, block, RI_AG + d - 1, z_peer(d)) for d in range(1, 8)]

    lax.fori_loop(9, POOL, fill, 0)
    for n in range(5, 8):
        og_forward(n)

    for c in ri_ag:
        c.wait_recv()
    ri_agx = send(rig.at[k, xl], rig.at[k, xl], RI_AGX, x_peer)
    for n in range(8):
        og_forward_x(n)
    ri_agx.wait_recv()
    ri_agc = send(rig.at[k], rig.at[k], RI_AGC, core_peer)

    get_ob.wait()
    for c in og_f:
        c.wait_recv()
    part = jnp.dot(
        ogg[0].reshape(TOKENS, HALF), pool[pl.ds(0, HALF), pl.ds(0, D_J)], preferred_element_type=F32
    ) + jnp.dot(
        ogg[1].reshape(TOKENS, HALF), pool[pl.ds(HALF, HALF), pl.ds(0, D_J)], preferred_element_type=F32
    )
    rop[...] = part
    ro_rs = [
        send(
            rop.at[pl.ds(pl.multiple_of(32 * lax.rem(row + d, 8), 32), 32), :],
            ror.at[d - 1], RO_RS + d - 1, row_peer(d),
        )
        for d in range(1, 8)
    ]
    lax.fori_loop(0, 4, fill, 0)

    ri_agc.wait_recv()
    for a in range(2):
        for b in range(2):
            for c in range(8):
                at = 128 * a + 64 * b + 16 * (c % 4)
                riv[at : at + 16, 512 * (c // 4) : 512 * (c // 4) + 512] = rig[a, b, c]

    def contract(m):
        return lax.dot_general(m, riv[...], (((1,), (1,)), ((), ())), preferred_element_type=F32)

    def early(n, carry):
        rows = pl.ds(pl.multiple_of(n * 2 * D_J, 2 * D_J), 2 * D_J)
        pst[rows, :] = contract(pool[rows, :]).astype(BF16)
        return carry

    lax.fori_loop(0, POOL // 4, early, 0)

    for c in ro_rs:
        c.wait_recv()
    total = rop[pl.ds(pl.multiple_of(32 * row, 32), 32), :]
    for d in range(1, 8):
        total = total + ror[d - 1]
    rog[row] = total.astype(BF16)
    block = rog.at[row]
    ro_ag = [send(block, block, RO_AG + d - 1, row_peer(d)) for d in range(1, 8)]

    lax.fori_loop(POOL // 4, POOL // 2, early, 0)
    ma[...] = weighted(POOL)
    for c in ro_ag:
        c.wait_recv()
    rot[...] = rog[...].reshape(TOKENS, D_J).T.astype(F32)

    def score(q, p):
        sc[pl.ds(q, 1), :] = jnp.sum(p * rot[...], axis=0, keepdims=True)

    late = QUERIES - POOL

    def finish(n, carry):
        for u, (src, dst) in enumerate(((ma, mb), (mb, ma))):
            q = POOL + 2 * n + u
            score(q, contract(src[...]))
            dst[...] = weighted(jnp.minimum(q + 1, QUERIES - 1))
            old = jnp.minimum(2 * n + u, POOL - 1)
            rows = pl.ds(pl.multiple_of(old * D_J, D_J), D_J)
            score(old, pst[rows, :].astype(F32))
        return carry

    lax.fori_loop(0, late // 2, finish, 0)

    parts = sc[...] * scl[...]
    token = lax.broadcasted_iota(jnp.int32, (TOKENS, 128), 0)
    lane = lax.broadcasted_iota(jnp.int32, (TOKENS, 128), 1)
    packed = jnp.zeros((8, 128), F32)
    for b in range(4):
        pick = jnp.where(lane == 16 * b + lax.div(token, 16), 1.0, 0.0)
        packed = packed + jnp.dot(
            parts[8 * b : 8 * b + 8], pick, precision=lax.Precision.HIGHEST, preferred_element_type=F32
        )
    ar_s[0] = packed
    c = send(ar_s.at[0], ar_r.at[0], AR_C, core_peer)
    c.wait_recv()
    packed = packed + ar_r[0]
    ar_s[1] = packed
    hops = [send(ar_s.at[1], ar_r.at[1 + n], AR_XY + n, xy_peer(d, e)) for n, (d, e) in enumerate(xy)]
    for c in hops:
        c.wait_recv()
    packed = packed + sum(ar_r[1 + n] for n in range(15))
    ar_s[2] = packed
    hops = [send(ar_s.at[2], ar_r.at[16 + d - 1], AR_Z + d - 1, z_peer(d)) for d in range(1, 8)]
    for c in hops:
        c.wait_recv()
    packed = packed + sum(ar_r[16 + n] for n in range(7))
    for b in range(4):
        out[8 * b : 8 * b + 8, :] = packed[:, 16 * b : 16 * b + 16]

    for c in started:
        c.wait_send()


def per_device(
    activations, out_grads, input_basis, output_basis, eigenvalues, query_inputs, query_outgrads
):
    any_, vmem = pl.BlockSpec(memory_space=pl.ANY), pl.BlockSpec(memory_space=pltpu.VMEM)
    scratch = [
        ((256, 256), BF16), ((256, D_I), BF16), ((512, D_I), BF16), ((512, D_J), BF16),
        ((2, 256, D_J), F32), ((D_J, D_I), F32), ((16, D_J, 128), F8), ((QUERIES, 128, D_I), F8),
        ((QUERIES, TOKENS), F32), ((POOL * D_J, D_I), BF16), ((D_J, D_I), BF16), ((D_J, D_I), BF16),
        ((POOL * D_J, TOKENS), BF16),
        ((256, D_I), F32), ((128, D_I), F32), ((128, D_I), F32),
        ((2, 64, D_I), BF16), ((64, D_I), BF16), ((8, 16, 512), BF16), ((8, 16, 512), F32),
        ((8, 16, 512), BF16), ((2, 2, 8, 16, 512), BF16), ((256, D_I), BF16),
        ((2, 8, HALF), F32), ((8, HALF), F32), ((2, 16, 16, HALF), BF16),
        ((256, D_J), F32), ((7, 32, D_J), F32), ((8, 32, D_J), BF16),
        ((D_J, TOKENS), F32), ((QUERIES, TOKENS), F32), ((3, 8, 128), F32), ((23, 8, 128), F32),
    ]
    return pl.pallas_call(
        kernel,
        out_shape=jax.ShapeDtypeStruct((QUERIES, SEQS), F32),
        in_specs=[any_, any_, vmem, any_, any_, any_, any_],
        out_specs=vmem,
        scratch_shapes=[pltpu.VMEM(s, t) for s, t in scratch]
        + [pltpu.SemaphoreType.DMA((9,)), pltpu.SemaphoreType.DMA((N_SEMS,)), pltpu.SemaphoreType.DMA((N_SEMS,))],
        compiler_params=pltpu.CompilerParams(
            collective_id=0, has_side_effects=True, vmem_limit_bytes=63 * 2**20
        ),
        name="influence",
    )(activations, input_basis, out_grads, query_inputs, query_outgrads, eigenvalues, output_basis)


def solution(mesh):
    in_specs = (
        P(None, "col"),
        P("col", "row"),
        P("col", "row"),
        P("row", "col"),
        P("row", "col"),
        P(None, "row"),
        P(None, "col"),
    )
    return jax.shard_map(
        per_device, mesh=mesh, in_specs=in_specs, out_specs=P(), check_vma=False
    )
```

time: 505 us -> 88.4 us (0.18)
  blocking collectives: 250 us -> 0 us
  matrix products: 208 us -> 0 us
  Pallas kernels: 0 us -> 86.8 us
  local copies, waits for them, and re-layouts: 27.2 us -> 1.39 us
  between operations: 13.4 us -> 0.01 us
    psum x3 -> x0, blocking collectives: 250 us -> none  [the longest x1 119 us: per_device(): rotated_in = lax.psum(in_terms, 'col').astype(jnp.bfloat16)]
    dot_general x26 -> x0, matrix products: 208 us -> none  [the longest x4 97 us: score_group(): jnp.einsum('qij,sij->qs', query_grad, scaled, preferred_element_type=jnp....]
    pallas_call x0 -> x1, Pallas kernels: none -> 86.8 us  [per_device(): pl.pallas_call(kernel, out_shape=jax.ShapeDtypeStruct((QUERIES, SEQS), F3...]
    while x1 -> x0, local copies, waits for them, and re-layouts: 26.2 us -> none  [per_device(): lax.map(score_group, (query_in, query_out)).reshape(QUERIES, SEQS)]
  transfers between devices with their start and end apart: 1 -> 0, of which waited for: 0 -> 0; matrix products, arithmetic and copies ran while one was open for 1% -> 0% of each run, Pallas kernels for 0% -> 0%
where the time goes in v1:
time: 88.4 us; the launch traced here: 88.2 us
  Pallas kernels  86.8 us (98%)
  local copies, waits for them, and re-layouts  1.39 us (2%)
    pallas_call x1, Pallas kernels, per_device(): pl.pallas_call(kernel, out_shape=jax.ShapeDtypeStruct((QUERIES, SEQS), F3...  86.8 us

profile of v1, /device:TPU:1, one launch (start us, length us, event | category | flops | bytes accessed | tf_op | source)
XLA Modules:
  0.0 88.2 jit_solution(17789509749413304730)
XLA Ops:
  0.0 86.8 %influence.1 = f32[32,16]{1,0:T(8,128)} custom-call(bf16[256,256]{1,0:T(8,128)(2,1)} %act.1, bf16[256,1024]{1,0:T(8,128)(2,1)} %ib.1, bf16[8,3584]{1,0:T(8,128)(2,1)} %og.1, bf16[512,1024]{1,0:T(8,128)(2,1)} %qi.1, bf16[512,896]{1,0:T(8,128)(2,1)} %qo.1, f32[1024,896]{1,0:T(8,128)} %eig.1, bf16[3584,896]{1,0:T(8,128)(2,1)} %ob.1), custom_call_target="tpu_custom_call" | custom-call | tf_op jit(solution)/shard_map/influence/pallas_call | solution.py:335
  86.8 1.4 %copy.8 = f32[32,16]{0,1:T(8,128)} copy(f32[32,16]{1,0:T(8,128)} %influence.1) | data formatting | bytes 4096 | tf_op jit(solution)/shard_map/influence/pallas_call | solution.py:335

commit v2 on v0

v2 whole, which is shorter than its diff:
```python
import functools

import jax
import jax.numpy as jnp
from jax import lax
from jax.experimental import pallas as pl
from jax.experimental.pallas import tpu as pltpu
from jax.sharding import PartitionSpec as P

MESH = pl.DeviceIdType.MESH
F32, BF16 = jnp.float32, jnp.bfloat16

D_I, D_J = 1024, 896
TOKENS, QUERIES, QTOK, SEQS = 256, 32, 16, 16
HALF = 1792
POOL = 16
PARTS = 2
WIDE = D_I // PARTS
DAMPING = 0.05
ORDER = (0, 1, 7, 2, 6, 3, 5, 4)

RI_CORE = 0
RI_X = RI_CORE + PARTS
RI_RS = RI_X + PARTS
RI_AG = RI_RS + 7 * PARTS
RI_AGX = RI_AG + 7 * PARTS
RI_AGC = RI_AGX + PARTS
OG_CORE = RI_AGC + PARTS
OG_Z = OG_CORE + 1
OG_X = OG_Z + 8
OG_C = OG_X + 8
RO_RS = OG_C + 16
RO_AG = RO_RS + 14
AR_C = RO_AG + 14
AR_XY = AR_C + 1
AR_Z = AR_XY + 15
N_SEMS = AR_Z + 7


def kernel(
    act, ib, og, qi, qo, eig, ob, out, spilled,
    act_v, ib_v, qi_v, qo_v, eig_v, wt, qa, pool, pst,
    rip, r1, acc1, s2, r2, s3, s3f, r3, rig, riv,
    ogx, ogr, ogg, rop, ros, ror, rog, rot, sc, ar_s, ar_r,
    lsem, osem, isem, ssem, rsem,
):
    row, col = lax.axis_index("row"), lax.axis_index("col")
    z, low = lax.div(col, 4), lax.rem(col, 4)
    xl, k = lax.div(low, 2), lax.rem(low, 2)
    core_peer = (row, col + 1 - 2 * k)
    x_col = z * 4 + lax.rem(low + 2, 4)
    x_peer = (row, x_col)

    def z_peer(d):
        return (row, lax.rem(z + d, 8) * 4 + low)

    def row_peer(d):
        return (lax.rem(row + d, 8), col)

    xy = [(d, e) for d in range(8) for e in range(2) if d or e]

    def xy_peer(d, e):
        return (lax.rem(row + d, 8), x_col if e else col)

    barrier = pltpu.get_barrier_semaphore()
    peers = [z_peer(d) for d in ORDER[:0:-1]] + [xy_peer(d, e) for d, e in xy] + [core_peer]
    for p in peers:
        pl.semaphore_signal(barrier, inc=1, device_id=p, device_id_type=MESH)

    started = []

    def send(src, dst, sem, peer):
        c = pltpu.make_async_remote_copy(
            src_ref=src, dst_ref=dst, send_sem=ssem.at[sem], recv_sem=rsem.at[sem],
            device_id=peer, device_id_type=MESH,
        )
        c.start()
        started.append(c)
        return c

    def fetch(src, dst, sem):
        c = pltpu.make_async_copy(src, dst, lsem.at[sem])
        c.start()
        return c

    ob_v = pool.at[pl.ds(0, 2 * HALF), pl.ds(0, D_J)]
    get_act = fetch(act, act_v, 0)
    get_ib = fetch(ib, ib_v, 1)
    get_eig = [fetch(eig.at[pl.ds(256 * c, 256)], eig_v.at[c % 2], 2 + c) for c in range(2)]
    get_qi = fetch(qi, qi_v, 6)
    get_qo = fetch(qo, qo_v, 7)

    own_og = og[...].astype(F32)
    ogx[0] = own_og[:, :HALF]
    ogx[1] = own_og[:, HALF:]

    get_act.wait()
    get_ib.wait()
    rip[...] = jnp.dot(act_v[...], ib_v[...], preferred_element_type=F32)

    pl.semaphore_wait(barrier, len(peers))

    def lanes(h):
        return pl.ds(WIDE * h, WIDE)

    og_c = send(ogx.at[1 - k], ogr, OG_CORE, core_peer)
    other_half = pl.ds(pl.multiple_of(128 - 128 * k, 128), 128)
    ri_c = [
        send(rip.at[other_half, lanes(h)], r1.at[:, lanes(h)], RI_CORE + h, core_peer)
        for h in range(PARTS)
    ]

    def slot_rows(slot, count=1):
        return pl.ds(pl.multiple_of(slot * D_J, D_J), count * D_J)

    def weighted(q, slot):
        group = lax.div(q, 8)
        tokens = qi_v[pl.ds(pl.multiple_of(group * 128, 128), 128), :]
        token = lax.broadcasted_iota(jnp.int32, tokens.shape, 0)
        own = jnp.where(lax.div(token, QTOK) == lax.rem(q, 8), tokens, jnp.zeros_like(tokens))
        for half in range(2):
            at = pl.ds(448 * half, 448)
            g = jnp.dot(qa[group, at, :], own, preferred_element_type=F32)
            rows = pl.ds(pl.multiple_of(slot * D_J + 448 * half, 448), 448)
            pool[rows, :] = (g.astype(BF16).astype(F32) * wt[at, :]).astype(BF16)

    def spill_copy(n, slot):
        return pltpu.make_async_copy(pool.at[slot_rows(slot), :], spilled.at[slot_rows(n), :], osem.at[n])

    def spill(n, carry):
        weighted(POOL + n, 4 + n)
        spill_copy(n, 4 + n).start()
        return carry

    def spill_last(n, carry):
        spill_copy(n - 12, n - 8).wait()
        weighted(POOL + n, n - 8)
        spill_copy(n, n - 8).start()
        return carry

    def fill_after_last(slot, carry):
        spill_copy(slot + 8, slot).wait()
        weighted(slot, slot)
        return carry

    def fill_after(slot, carry):
        spill_copy(slot - 4, slot).wait()
        weighted(slot, slot)
        return carry

    def fill(slot, carry):
        weighted(slot, slot)
        return carry

    for h in range(PARTS):
        ri_c[h].wait_recv()
    acc = rip[pl.ds(pl.multiple_of(128 * k, 128), 128), :] + r1[...]
    acc1[...] = acc
    s2[0] = acc[:64].astype(BF16)
    s2[1] = acc[64:].astype(BF16)
    ri_x = [
        send(s2.at[1 - xl, :, lanes(h)], r2.at[:, lanes(h)], RI_X + h, x_peer) for h in range(PARTS)
    ]

    og_c.wait_recv()
    mine = ogx[k]
    other = ogr[...]
    first = jnp.where(k == 0, mine, other)
    second = jnp.where(k == 0, other, mine)
    ogg[k, 0, xl] = jnp.concatenate([first, second], axis=0).astype(BF16)

    def og_send(n):
        return send(ogg.at[k, 0, xl], ogg.at[k, n, xl], OG_Z + n, z_peer(ORDER[n]))

    def og_pass(n, to, d):
        block = ogg.at[k, n, xl]
        og_z[to] = send(block, ogg.at[k, to, xl], OG_Z + to, z_peer(d))

    og_z = {n: og_send(n) for n in range(1, 5)}
    og_x, og_f = {}, {}

    def og_forward(n):
        if n:
            og_z[n].wait_recv()
        block = ogg.at[k, n, xl]
        if n not in (1, 2):
            og_x[n] = send(block, block, OG_X + n, x_peer)
        og_f[2 * n] = send(block, block, OG_C + 2 * n, core_peer)

    def og_forward_x(n):
        og_x[n].wait_recv()
        block = ogg.at[k, n, 1 - xl]
        og_f[2 * n + 1] = send(block, block, OG_C + 2 * n + 1, core_peer)
        if n == 0:
            for to, d in ((1, 1), (2, 7)):
                og_x[to] = send(block, ogg.at[k, to, 1 - xl], OG_X + to, z_peer(d))

    og_forward(0)
    for c in range(4):
        get_eig[c].wait()
        wt[:, pl.ds(256 * c, 256)] = 1.0 / (eig_v[c % 2].T + DAMPING)
        if c < 2:
            get_eig.append(fetch(eig.at[pl.ds(256 * (c + 2), 256)], eig_v.at[c % 2], 4 + c))
    get_ob = fetch(ob, ob_v, 8)
    get_qi.wait()
    get_qo.wait()
    for group in range(4):
        qa[group] = qo_v[128 * group : 128 * group + 128, :].T

    lax.fori_loop(0, 3, spill, 0)

    ri_rs = []
    for h in range(PARTS):
        ri_x[h].wait_recv()
        acc = acc1[pl.ds(pl.multiple_of(64 * xl, 64), 64), lanes(h)] + r2[:, lanes(h)].astype(F32)
        for c in range(8):
            at = WIDE // 2 * (c // 4)
            piece = acc[16 * (c % 4) : 16 * (c % 4) + 16, at : at + WIDE // 2]
            s3f[h, c] = piece
            s3[h, c] = piece.astype(BF16)
        ri_rs.append(
            [
                send(s3.at[h, lax.rem(z + d, 8)], r3.at[h, d], RI_RS + 7 * h + d - 1, z_peer(d))
                for d in ORDER[:0:-1]
            ]
        )
    og_forward_x(0)
    lax.fori_loop(3, 6, spill, 0)
    for n in range(3, 5):
        og_forward(n)
    og_pass(3, 5, 1)
    og_pass(4, 6, 7)
    og_pass(3, 7, 2)
    for n in range(1, 3):
        og_forward(n)

    lax.fori_loop(6, 12, spill, 0, unroll=2)
    for n in range(1, 4):
        og_forward_x(n)
    lax.fori_loop(12, 16, spill_last, 0, unroll=2)

    ri_ag = []
    for h in range(PARTS):
        for c in ri_rs[h]:
            c.wait_recv()
        total = s3f[h, z]
        for d in range(1, 8):
            total = total + r3[h, d].astype(F32)
        rig[k, h, xl, z] = total.astype(BF16)
        block = rig.at[k, h, xl, z]
        ri_ag.append([send(block, block, RI_AG + 7 * h + d - 1, z_peer(d)) for d in ORDER[:0:-1]])

    lax.fori_loop(8, 10, fill_after, 0, unroll=2)
    for n in range(5, 8):
        og_forward(n)
    og_forward_x(4)
    lax.fori_loop(10, 14, fill_after, 0, unroll=2)

    def ro_start(c):
        for n in range(8 * c, 8 * c + 8):
            og_f[n].wait_recv()
        tokens = [ogg[a, 4 * c : 4 * c + 4].reshape(128, HALF) for a in range(2)]
        part = jnp.dot(tokens[0], pool[pl.ds(0, HALF), pl.ds(0, D_J)], preferred_element_type=F32)
        part = part + jnp.dot(
            tokens[1], pool[pl.ds(HALF, HALF), pl.ds(0, D_J)], preferred_element_type=F32
        )
        rop[c] = part.reshape(8, 16, D_J)
        ros[c] = part.reshape(8, 16, D_J).astype(BF16)
        return [
            send(ros.at[c, lax.rem(row + d, 8)], ror.at[c, d - 1], RO_RS + 7 * c + d - 1, row_peer(d))
            for d in range(1, 8)
        ]

    def ro_sum(c):
        for f in ro_rs[c]:
            f.wait_recv()
        total = rop[c, row]
        for d in range(1, 8):
            total = total + ror[c, d - 1].astype(F32)
        n = 4 * c + lax.div(row, 2)
        far = lax.div(n + 1, 2)
        source = lax.rem(jnp.where(lax.rem(n, 2) == 1, z + 8 - far, z + far), 8)
        seq = 2 * source + lax.rem(row, 2)
        rog[seq] = total.astype(BF16)
        block = rog.at[seq]
        return [send(block, block, RO_AG + 7 * c + d - 1, row_peer(d)) for d in range(1, 8)]

    get_ob.wait()
    ro_rs = [ro_start(0)]
    lax.fori_loop(14, 16, fill_after, 0, unroll=2)
    lax.fori_loop(4, 6, fill_after_last, 0, unroll=2)

    ri_agx = []
    for h in range(PARTS):
        for c in ri_ag[h]:
            c.wait_recv()
        block = rig.at[k, h, xl]
        ri_agx.append(send(block, block, RI_AGX + h, x_peer))

    lax.fori_loop(6, 8, fill_after_last, 0, unroll=2)
    for n in range(5, 8):
        og_forward_x(n)
    ri_agc = []
    for h in range(PARTS):
        ri_agx[h].wait_recv()
        ri_agc.append(send(rig.at[k, h], rig.at[k, h], RI_AGC + h, core_peer))

    ro_rs.append(ro_start(1))
    lax.fori_loop(0, 4, fill, 0, unroll=2)

    for h in range(PARTS):
        ri_agc[h].wait_recv()
        for a in range(2):
            for b in range(2):
                for c in range(8):
                    at = 128 * a + 64 * b + 16 * (c % 4)
                    lane = WIDE * h + WIDE // 2 * (c // 4)
                    riv[at : at + 16, lane : lane + WIDE // 2] = rig[a, h, b, c]

    def fetch_four(n):
        rows = slot_rows(4 * n, 4)
        return pltpu.make_async_copy(spilled.at[rows, :], pool.at[rows, :], isem.at[n])

    def contract(n, to):
        for part in range(4):
            pst[slot_rows(4 * to + part), :] = lax.dot_general(
                pool[slot_rows(4 * n + part), :], riv[...], (((1,), (1,)), ((), ())),
                preferred_element_type=F32,
            ).astype(BF16)

    def keep(n, carry):
        contract(n, n)
        fetch_four(n).start()
        return carry

    def keep_fetched(n, carry):
        fetch_four(n).wait()
        contract(n, n + POOL // 4)
        return carry

    lax.fori_loop(0, 1, keep, 0)
    ro_ag = [ro_sum(0)]
    lax.fori_loop(1, 3, keep, 0)
    ro_ag.append(ro_sum(1))
    lax.fori_loop(3, 4, keep, 0)
    lax.fori_loop(0, 3, keep_fetched, 0)

    for c in range(2):
        for f in ro_ag[c]:
            f.wait_recv()
    rot[...] = rog[...].reshape(TOKENS, D_J).T.astype(F32)

    def score(q, p):
        sc[pl.ds(q, 1), :] = jnp.sum(p * rot[...], axis=0, keepdims=True)

    fetch_four(3).wait()

    def last(part, carry):
        p = lax.dot_general(
            pool[slot_rows(12 + part), :], riv[...], (((1,), (1,)), ((), ())), preferred_element_type=F32
        )
        for u in range(7):
            q = 7 * part + u
            score(q, pst[slot_rows(q), :].astype(F32))
        score(28 + part, p)
        return carry

    lax.fori_loop(0, 4, last, 0)

    parts = sc[...]
    high = parts.astype(BF16)
    rest = parts - high.astype(F32)
    middle = rest.astype(BF16)
    low_bits = (rest - middle.astype(F32)).astype(BF16)
    token = lax.broadcasted_iota(jnp.int32, (TOKENS, 128), 0)
    lane = lax.broadcasted_iota(jnp.int32, (TOKENS, 128), 1)
    pick = jnp.where(lane == lax.div(token, 16), 1.0, 0.0).astype(BF16)
    sums = jnp.dot(
        jnp.concatenate([high, middle, low_bits], axis=0), pick, preferred_element_type=F32
    )
    sums = sums[:32] + sums[32:64] + sums[64:]
    packed = sums[:8]
    for b in range(1, 4):
        packed = packed + pltpu.roll(sums[8 * b : 8 * b + 8], 16 * b, axis=1)
    ar_s[0] = packed
    c = send(ar_s.at[0], ar_r.at[0], AR_C, core_peer)
    c.wait_recv()
    packed = packed + ar_r[0]
    ar_s[1] = packed
    hops = [send(ar_s.at[1], ar_r.at[1 + n], AR_XY + n, xy_peer(d, e)) for n, (d, e) in enumerate(xy)]
    for c in hops:
        c.wait_recv()
    packed = packed + sum(ar_r[1 + n] for n in range(15))
    ar_s[2] = packed
    hops = [send(ar_s.at[2], ar_r.at[16 + d - 1], AR_Z + d - 1, z_peer(d)) for d in range(1, 8)]
    for c in hops:
        c.wait_recv()
    packed = packed + sum(ar_r[16 + n] for n in range(7))
    for b in range(4):
        out[8 * b : 8 * b + 8, :] = packed[:, 16 * b : 16 * b + 16]

    for c in started:
        c.wait_send()


def per_device(
    activations, out_grads, input_basis, output_basis, eigenvalues, query_inputs, query_outgrads
):
    any_, vmem = pl.BlockSpec(memory_space=pl.ANY), pl.BlockSpec(memory_space=pltpu.VMEM)
    piece = (16, WIDE // 2)
    scratch = [
        ((256, 256), BF16), ((256, D_I), BF16), ((512, D_I), BF16), ((512, D_J), BF16),
        ((2, 256, D_J), F32), ((D_J, D_I), F32), ((4, D_J, 128), BF16),
        ((POOL * D_J, D_I), BF16), ((28 * D_J, TOKENS), BF16),
        ((256, D_I), F32), ((128, D_I), F32), ((128, D_I), F32),
        ((2, 64, D_I), BF16), ((64, D_I), BF16), ((PARTS, 8, *piece), BF16), ((PARTS, 8, *piece), F32),
        ((PARTS, 8, *piece), BF16), ((2, PARTS, 2, 8, *piece), BF16), ((256, D_I), BF16),
        ((2, 8, HALF), F32), ((8, HALF), F32), ((2, 8, 2, 16, HALF), BF16),
        ((2, 8, 16, D_J), F32), ((2, 8, 16, D_J), BF16), ((2, 7, 16, D_J), BF16), ((16, 16, D_J), BF16),
        ((D_J, TOKENS), F32), ((QUERIES, TOKENS), F32), ((3, 8, 128), F32), ((23, 8, 128), F32),
    ]
    dma = pltpu.SemaphoreType.DMA
    scores, _ = pl.pallas_call(
        kernel,
        out_shape=[
            jax.ShapeDtypeStruct((QUERIES, SEQS), F32),
            jax.ShapeDtypeStruct(((QUERIES - POOL) * D_J, D_I), BF16),
        ],
        in_specs=[any_, any_, vmem, any_, any_, any_, any_],
        out_specs=[vmem, any_],
        scratch_shapes=[pltpu.VMEM(s, t) for s, t in scratch]
        + [dma((9,)), dma((16,)), dma((4,)), dma((N_SEMS,)), dma((N_SEMS,))],
        compiler_params=pltpu.CompilerParams(
            collective_id=0, has_side_effects=True, vmem_limit_bytes=63 * 2**20
        ),
        name="influence",
    )(activations, input_basis, out_grads, query_inputs, query_outgrads, eigenvalues, output_basis)
    return scores


def solution(mesh):
    in_specs = (
        P(None, "col"),
        P("col", "row"),
        P("col", "row"),
        P("row", "col"),
        P("row", "col"),
        P(None, "row"),
        P(None, "col"),
    )
    return jax.shard_map(
        per_device, mesh=mesh, in_specs=in_specs, out_specs=P(), check_vma=False
    )
```

time: 505 us -> 78.5 us (0.16)
  blocking collectives: 250 us -> 0 us
  matrix products: 208 us -> 0 us
  Pallas kernels: 0 us -> 76.9 us
  local copies, waits for them, and re-layouts: 27.2 us -> 1.39 us
  between operations: 13.4 us -> 0.01 us
    psum x3 -> x0, blocking collectives: 250 us -> none  [the longest x1 119 us: per_device(): rotated_in = lax.psum(in_terms, 'col').astype(jnp.bfloat16)]
    dot_general x26 -> x0, matrix products: 208 us -> none  [the longest x4 97 us: score_group(): jnp.einsum('qij,sij->qs', query_grad, scaled, preferred_element_type=jnp....]
    pallas_call x0 -> x1, Pallas kernels: none -> 76.9 us  [per_device(): pl.pallas_call(kernel, out_shape=[jax.ShapeDtypeStruct((QUERIES, SEQS), F...]
    while x1 -> x0, local copies, waits for them, and re-layouts: 26.2 us -> none  [per_device(): lax.map(score_group, (query_in, query_out)).reshape(QUERIES, SEQS)]
  transfers between devices with their start and end apart: 1 -> 0, of which waited for: 0 -> 0; matrix products, arithmetic and copies ran while one was open for 1% -> 0% of each run, Pallas kernels for 0% -> 0%
where the time goes in v2:
time: 78.5 us; the launch traced here: 78.3 us
  Pallas kernels  76.9 us (98%)
  local copies, waits for them, and re-layouts  1.39 us (2%)
    pallas_call x1, Pallas kernels, per_device(): pl.pallas_call(kernel, out_shape=[jax.ShapeDtypeStruct((QUERIES, SEQS), F...  76.9 us

profile of v2, /device:TPU:1, one launch (start us, length us, event | category | flops | bytes accessed | tf_op | source)
XLA Modules:
  0.0 78.3 jit_solution(6816804770780449618)
XLA Ops:
  0.0 76.9 %influence.1 = (f32[32,16]{1,0:T(8,128)}, bf16[14336,1024]{1,0:T(8,128)(2,1)}) custom-call(bf16[256,256]{1,0:T(8,128)(2,1)} %act.1, bf16[256,1024]{1,0:T(8,128)(2,1)} %ib.1, bf16[8,3584]{1,0:T(8,128)(2,1)} %og.1, bf16[512,1024]{1,0:T(8,128)(2,1)} %qi.1, bf16[512,896]{1,0:T(8,128)(2,1)} %qo.1, f32[1024,896]{1,0:T(8,128)} %eig.1, bf16[3584,896]{1,0:T(8,128)(2,1)} %ob.1), custom_call_target="tpu_custom_call" | custom-call | tf_op jit(solution)/shard_map/influence/pallas_call | solution.py:423
  76.9 1.4 %copy.8 = f32[32,16]{0,1:T(8,128)} copy(f32[32,16]{1,0:T(8,128)} %get-tuple-element.6) | data formatting | bytes 4096 | tf_op jit(solution)/shard_map/influence/pallas_call | solution.py:423

commit v3 on v2

--- a/solution.py
+++ b/solution.py
@@ -152,15 +152,14 @@
         weighted(slot, slot)
         return carry
 
+    ri_x = []
     for h in range(PARTS):
         ri_c[h].wait_recv()
-    acc = rip[pl.ds(pl.multiple_of(128 * k, 128), 128), :] + r1[...]
-    acc1[...] = acc
-    s2[0] = acc[:64].astype(BF16)
-    s2[1] = acc[64:].astype(BF16)
-    ri_x = [
-        send(s2.at[1 - xl, :, lanes(h)], r2.at[:, lanes(h)], RI_X + h, x_peer) for h in range(PARTS)
-    ]
+        acc = rip[pl.ds(pl.multiple_of(128 * k, 128), 128), lanes(h)] + r1[:, lanes(h)]
+        acc1[:, lanes(h)] = acc
+        s2[0, :, lanes(h)] = acc[:64].astype(BF16)
+        s2[1, :, lanes(h)] = acc[64:].astype(BF16)
+        ri_x.append(send(s2.at[1 - xl, :, lanes(h)], r2.at[:, lanes(h)], RI_X + h, x_peer))
 
     og_c.wait_recv()
     mine = ogx[k]
@@ -206,8 +205,6 @@
     get_qo.wait()
     for group in range(4):
         qa[group] = qo_v[128 * group : 128 * group + 128, :].T
-
-    lax.fori_loop(0, 3, spill, 0)
 
     ri_rs = []
     for h in range(PARTS):
@@ -225,7 +222,7 @@
             ]
         )
     og_forward_x(0)
-    lax.fori_loop(3, 6, spill, 0)
+    lax.fori_loop(0, 4, spill, 0, unroll=4)
     for n in range(3, 5):
         og_forward(n)
     og_pass(3, 5, 1)
@@ -234,10 +231,9 @@
     for n in range(1, 3):
         og_forward(n)
 
-    lax.fori_loop(6, 12, spill, 0, unroll=2)
+    lax.fori_loop(4, 12, spill, 0, unroll=4)
     for n in range(1, 4):
         og_forward_x(n)
-    lax.fori_loop(12, 16, spill_last, 0, unroll=2)
 
     ri_ag = []
     for h in range(PARTS):
@@ -250,11 +246,11 @@
         block = rig.at[k, h, xl, z]
         ri_ag.append([send(block, block, RI_AG + 7 * h + d - 1, z_peer(d)) for d in ORDER[:0:-1]])
 
-    lax.fori_loop(8, 10, fill_after, 0, unroll=2)
+    lax.fori_loop(12, 16, spill_last, 0, unroll=4)
     for n in range(5, 8):
         og_forward(n)
     og_forward_x(4)
-    lax.fori_loop(10, 14, fill_after, 0, unroll=2)
+    lax.fori_loop(8, 12, fill_after, 0, unroll=4)
 
     def ro_start(c):
         for n in range(8 * c, 8 * c + 8):
@@ -287,8 +283,6 @@
 
     get_ob.wait()
     ro_rs = [ro_start(0)]
-    lax.fori_loop(14, 16, fill_after, 0, unroll=2)
-    lax.fori_loop(4, 6, fill_after_last, 0, unroll=2)
 
     ri_agx = []
     for h in range(PARTS):
@@ -297,16 +291,16 @@
         block = rig.at[k, h, xl]
         ri_agx.append(send(block, block, RI_AGX + h, x_peer))
 
-    lax.fori_loop(6, 8, fill_after_last, 0, unroll=2)
+    lax.fori_loop(12, 16, fill_after, 0, unroll=4)
     for n in range(5, 8):
         og_forward_x(n)
+    ro_rs.append(ro_start(1))
+    lax.fori_loop(4, 8, fill_after_last, 0, unroll=4)
     ri_agc = []
     for h in range(PARTS):
         ri_agx[h].wait_recv()
         ri_agc.append(send(rig.at[k, h], rig.at[k, h], RI_AGC + h, core_peer))
-
-    ro_rs.append(ro_start(1))
-    lax.fori_loop(0, 4, fill, 0, unroll=2)
+    lax.fori_loop(0, 4, fill, 0, unroll=4)
 
     for h in range(PARTS):
         ri_agc[h].wait_recv()
@@ -340,10 +334,10 @@
 
     lax.fori_loop(0, 1, keep, 0)
     ro_ag = [ro_sum(0)]
-    lax.fori_loop(1, 3, keep, 0)
+    lax.fori_loop(1, 2, keep, 0)
     ro_ag.append(ro_sum(1))
-    lax.fori_loop(3, 4, keep, 0)
-    lax.fori_loop(0, 3, keep_fetched, 0)
+    lax.fori_loop(2, 4, keep, 0)
+    lax.fori_loop(0, 2, keep_fetched, 0)
 
     for c in range(2):
         for f in ro_ag[c]:
@@ -353,19 +347,20 @@
     def score(q, p):
         sc[pl.ds(q, 1), :] = jnp.sum(p * rot[...], axis=0, keepdims=True)
 
+    fetch_four(2).wait()
     fetch_four(3).wait()
 
     def last(part, carry):
         p = lax.dot_general(
-            pool[slot_rows(12 + part), :], riv[...], (((1,), (1,)), ((), ())), preferred_element_type=F32
+            pool[slot_rows(8 + part), :], riv[...], (((1,), (1,)), ((), ())), preferred_element_type=F32
         )
-        for u in range(7):
-            q = 7 * part + u
+        for u in range(3):
+            q = 3 * part + u
             score(q, pst[slot_rows(q), :].astype(F32))
-        score(28 + part, p)
-        return carry
-
-    lax.fori_loop(0, 4, last, 0)
+        score(24 + part, p)
+        return carry
+
+    lax.fori_loop(0, 8, last, 0, unroll=2)
 
     parts = sc[...]
     high = parts.astype(BF16)
@@ -387,7 +382,11 @@
     c.wait_recv()
     packed = packed + ar_r[0]
     ar_s[1] = packed
+    earlier = list(started)
+    started.clear()
     hops = [send(ar_s.at[1], ar_r.at[1 + n], AR_XY + n, xy_peer(d, e)) for n, (d, e) in enumerate(xy)]
+    for c in earlier:
+        c.wait_send()
     for c in hops:
         c.wait_recv()
     packed = packed + sum(ar_r[1 + n] for n in range(15))
@@ -411,7 +410,7 @@
     scratch = [
         ((256, 256), BF16), ((256, D_I), BF16), ((512, D_I), BF16), ((512, D_J), BF16),
         ((2, 256, D_J), F32), ((D_J, D_I), F32), ((4, D_J, 128), BF16),
-        ((POOL * D_J, D_I), BF16), ((28 * D_J, TOKENS), BF16),
+        ((POOL * D_J, D_I), BF16), ((24 * D_J, TOKENS), BF16),
         ((256, D_I), F32), ((128, D_I), F32), ((128, D_I), F32),
         ((2, 64, D_I), BF16), ((64, D_I), BF16), ((PARTS, 8, *piece), BF16), ((PARTS, 8, *piece), F32),
         ((PARTS, 8, *piece), BF16), ((2, PARTS, 2, 8, *piece), BF16), ((256, D_I), BF16),

time: 78.5 us -> 75.2 us (0.958)
  Pallas kernels: 76.9 us -> 73.3 us
    pallas_call x1, Pallas kernels: 76.9 us -> 73.3 us  [per_device(): pl.pallas_call(kernel, out_shape=[jax.ShapeDtypeStruct((QUERIES, SEQS), F...]
where the time goes in v3:
time: 75.2 us; the launch traced here: 74.7 us
  Pallas kernels  73.3 us (97%)
  local copies, waits for them, and re-layouts  1.39 us (2%)
    pallas_call x1, Pallas kernels, per_device(): pl.pallas_call(kernel, out_shape=[jax.ShapeDtypeStruct((QUERIES, SEQS), F...  73.3 us

profile of v3, /device:TPU:1, one launch (start us, length us, event | category | flops | bytes accessed | tf_op | source)
XLA Modules:
  0.0 74.7 jit_solution(268288378332868182)
XLA Ops:
  0.0 73.3 %influence.1 = (f32[32,16]{1,0:T(8,128)}, bf16[14336,1024]{1,0:T(8,128)(2,1)}) custom-call(bf16[256,256]{1,0:T(8,128)(2,1)} %act.1, bf16[256,1024]{1,0:T(8,128)(2,1)} %ib.1, bf16[8,3584]{1,0:T(8,128)(2,1)} %og.1, bf16[512,1024]{1,0:T(8,128)(2,1)} %qi.1, bf16[512,896]{1,0:T(8,128)(2,1)} %qo.1, f32[1024,896]{1,0:T(8,128)} %eig.1, bf16[3584,896]{1,0:T(8,128)(2,1)} %ob.1), custom_call_target="tpu_custom_call" | custom-call | tf_op jit(solution)/shard_map/influence/pallas_call | solution.py:422
  73.3 1.4 %copy.8 = f32[32,16]{0,1:T(8,128)} copy(f32[32,16]{1,0:T(8,128)} %get-tuple-element.6) | data formatting | bytes 4096 | tf_op jit(solution)/shard_map/influence/pallas_call | solution.py:422

commit v4 on v3

--- a/solution.py
+++ b/solution.py
@@ -152,6 +152,14 @@
         weighted(slot, slot)
         return carry
 
+    def invert(begin, end):
+        for c in range(begin, end):
+            get_eig[c].wait()
+            wt[:, pl.ds(256 * c, 256)] = 1.0 / (eig_v[c % 2].T + DAMPING)
+            if c < 2:
+                get_eig.append(fetch(eig.at[pl.ds(256 * (c + 2), 256)], eig_v.at[c % 2], 4 + c))
+
+    invert(0, 2)
     ri_x = []
     for h in range(PARTS):
         ri_c[h].wait_recv()
@@ -195,11 +203,7 @@
                 og_x[to] = send(block, ogg.at[k, to, 1 - xl], OG_X + to, z_peer(d))
 
     og_forward(0)
-    for c in range(4):
-        get_eig[c].wait()
-        wt[:, pl.ds(256 * c, 256)] = 1.0 / (eig_v[c % 2].T + DAMPING)
-        if c < 2:
-            get_eig.append(fetch(eig.at[pl.ds(256 * (c + 2), 256)], eig_v.at[c % 2], 4 + c))
+    invert(2, 4)
     get_ob = fetch(ob, ob_v, 8)
     get_qi.wait()
     get_qo.wait()

time: 75.2 us -> 75.2 us (level)
  no operation moved by 1% of the time
where the time goes in v4:
time: 75.2 us; the launch traced here: 74.7 us
  Pallas kernels  73.3 us (97%)
  local copies, waits for them, and re-layouts  1.39 us (2%)
    pallas_call x1, Pallas kernels, per_device(): pl.pallas_call(kernel, out_shape=[jax.ShapeDtypeStruct((QUERIES, SEQS), F...  73.3 us

profile of v4, /device:TPU:1, one launch (start us, length us, event | category | flops | bytes accessed | tf_op | source)
XLA Modules:
  0.0 74.7 jit_solution(11336661866884040988)
XLA Ops:
  0.0 73.3 %influence.1 = (f32[32,16]{1,0:T(8,128)}, bf16[14336,1024]{1,0:T(8,128)(2,1)}) custom-call(bf16[256,256]{1,0:T(8,128)(2,1)} %act.1, bf16[256,1024]{1,0:T(8,128)(2,1)} %ib.1, bf16[8,3584]{1,0:T(8,128)(2,1)} %og.1, bf16[512,1024]{1,0:T(8,128)(2,1)} %qi.1, bf16[512,896]{1,0:T(8,128)(2,1)} %qo.1, f32[1024,896]{1,0:T(8,128)} %eig.1, bf16[3584,896]{1,0:T(8,128)(2,1)} %ob.1), custom_call_target="tpu_custom_call" | custom-call | tf_op jit(solution)/shard_map/influence/pallas_call | solution.py:426
  73.3 1.4 %copy.8 = f32[32,16]{0,1:T(8,128)} copy(f32[32,16]{1,0:T(8,128)} %get-tuple-element.6) | data formatting | bytes 4096 | tf_op jit(solution)/shard_map/influence/pallas_call | solution.py:426
